TPU v7x, 32 devices: a whole 2x2x4 slice. The times are simulated.
32 devices in a mesh: parts: 2 (over x), space: 16 (over z, y, core).
Axes of the slice: x: 2, y: 2, z: 4, core: 2. Of those that a mesh axis runs over, the one named last changes fastest.
Arguments:
- obs: bfloat16 [192, 256, 512], P(('parts', 'space')), parts along dimension 0, may hold values from -16 to 16
- counts: int32 [192], P(('parts', 'space')), parts along dimension 0, may hold values from 64 to 256, as said below
- neighbours: int32 [192, 4], P(('parts', 'space')), parts along dimension 0, may hold values from -1 to 94, as said below
- krig: bfloat16 [192, 4, 256, 256], P(('parts', 'space')), parts along dimension 0, may hold values from -0.1875 to 0.1875
- knot_load: bfloat16 [192, 256, 2048], P(('parts', 'space')), parts along dimension 0, may hold values from -0.1875 to 0.1875
- knot_values: bfloat16 [4096, 512], P(('parts', 'space')), parts along dimension 0, may hold values from -6 to 6
- whiten: bfloat16 [192, 256, 256], P(('parts', 'space')), parts along dimension 0, may hold values from -1 to 2, as said below
- noise_var: float32 [512], replicated, may hold values from 0.2 to 1
Outputs:
- posterior: bfloat16 [192, 256, 512], P(('parts', 'space')), parts along dimension 0
- average_loglik: float32 [1024], P('parts'), parts along dimension 0
- knot_score: float32 [4096, 512], P(('parts', 'space')), parts along dimension 0
There are 2 independent parts, one for each index of `parts`. A program takes and returns all parts, laid end to end along the dimension named above; an argument that names none is the same for every part. Nothing has to cross between parts.
Inputs may be any that keep to these rules, and one draw needn't show every extreme that they name: `neighbours`: entry 0 of block b's list is b - 1 (-1 for block 0); the other entries are distinct ids from b - 9 to b - 2, or -1. A block's valid points are its first counts[b] points; the rest is padding. `whiten`: each block's factor is lower triangular with a positive diagonal.
All inputs are finite; a program needn't handle non-finite values.
Results may differ from a plain program's by a relative error of at most 0.00105.
The roundings to bfloat16 on the way count: a program that leaves them out, or rounds other values in their place, can miss the bound.
Values may be sent and summed in bfloat16 or wider, within the bound.
A program may use at most 128 MiB of HBM per device.

v0:
```python
import jax
import jax.numpy as jnp
from jax import lax
from jax.sharding import PartitionSpec as P


def from_behind(x, axis, by):
    count = lax.axis_size(axis)
    pairs = [(i, i + by) for i in range(count) if 0 <= i + by < count]
    return lax.ppermute(x, axis, pairs)


def local(obs, counts, neighbours, krig, knot_load, knot_values, whiten, noise_var):
    slot_count = obs.shape[0]
    point_count = obs.shape[1]
    field_count = obs.shape[2]
    knot_count = knot_load.shape[2]
    point_mask = (jnp.arange(point_count)[None, :] < counts[:, None]).astype(jnp.float32)
    spread_mask = point_mask[:, :, None]
    masked = (obs.astype(jnp.float32) * spread_mask).astype(jnp.bfloat16)
    pieces = []
    for distance in (2, 1):
        outgoing = masked if distance == 1 else masked
        pieces.append(from_behind(outgoing, "space", distance))
    window = jnp.concatenate(pieces + [masked], axis=0)
    window_length = window.shape[0]
    anchor = lax.axis_index("space") * slot_count - slot_count - slot_count
    usable = neighbours >= 0
    window_ids = jnp.where(usable, neighbours - anchor, 0)
    near_rows = jnp.where(usable[:, :, None, None], window[window_ids], jnp.zeros((), jnp.bfloat16))
    predicted = jnp.einsum("skij,skjt->sit", krig, near_rows, preferred_element_type=jnp.float32)
    flat_load = knot_load.reshape(slot_count * point_count, knot_count)
    columns = flat_load
    coarse = jnp.dot(
        columns,
        lax.all_gather(knot_values, "space", axis=0, tiled=True),
        preferred_element_type=jnp.float32,
    )
    residual = (
        spread_mask * (masked.astype(jnp.float32) - predicted - coarse.reshape(obs.shape))
    ).astype(jnp.bfloat16)
    whitened = spread_mask * jnp.einsum(
        "sij,sjt->sit", whiten, residual, preferred_element_type=jnp.float32
    )
    whitened_half = whitened.astype(jnp.bfloat16)
    adjoint = spread_mask * jnp.einsum(
        "sji,sjt->sit", whiten, whitened_half, preferred_element_type=jnp.float32
    )
    adjoint_half = adjoint.astype(jnp.bfloat16)
    diagonal = jnp.diagonal(whiten, axis1=1, axis2=2).astype(jnp.float32)
    totals = lax.psum(
        (
            jnp.sum(whitened * whitened, axis=(0, 1)),
            jnp.sum(point_mask * jnp.log(diagonal)),
            jnp.sum(counts).astype(jnp.float32),
        ),
        "space",
    )
    average_loglik = (totals[1] - 0.5 * totals[0]) / totals[2]
    flat_adjoint = adjoint_half.reshape(slot_count * point_count, field_count)
    columns = flat_load
    knot_score = lax.psum_scatter(
        lax.dot_general(
            columns, flat_adjoint, (((0,), (0,)), ((), ())), preferred_element_type=jnp.float32
        ),
        "space",
        scatter_dimension=0,
        tiled=True,
    )
    transposed = jnp.einsum(
        "skij,sit->skjt", krig, adjoint_half, preferred_element_type=jnp.float32
    )
    target_ids = jnp.where(usable, window_ids, window_length)
    window_sums = (
        jnp.zeros((window_length, point_count, field_count), jnp.float32)
        .at[target_ids.reshape(-1)]
        .add(transposed.reshape(-1, point_count, field_count), mode="drop")
    )
    returned = window_sums.astype(jnp.bfloat16)
    incoming = returned[slot_count + slot_count :].astype(jnp.float32)
    for distance in (2, 1):
        offset = 0 if distance == 2 else slot_count
        extent = slot_count if distance == 2 else slot_count
        received = from_behind(returned[offset : offset + extent], "space", -distance)
        incoming = incoming.at[slot_count - extent :].add(received.astype(jnp.float32))
    precision_resid = spread_mask * (adjoint - incoming)
    posterior = (masked.astype(jnp.float32) - noise_var[None, None, :] * precision_resid).astype(
        jnp.bfloat16
    )
    return (posterior, average_loglik, knot_score)


def solution(mesh):
    in_specs = (
        P(("parts", "space"), None, None),
        P(("parts", "space")),
        P(("parts", "space"), None),
        P(("parts", "space"), None, None, None),
        P(("parts", "space"), None, None),
        P(("parts", "space"), None),
        P(("parts", "space"), None, None),
        P(),
    )
    out_specs = (P(("parts", "space"), None, None), P("parts"), P(("parts", "space"), None))
    return jax.shard_map(local, mesh=mesh, in_specs=in_specs, out_specs=out_specs, check_vma=False)
```

profile of v0, /device:TPU:0, one launch (start us, length us, event | category | flops | bytes accessed | tf_op | source)
XLA Modules:
  0.0 278.5 jit_solution(10744897955229781012)
XLA Ops:
  7.2 0.0 copy-start
  7.2 0.0 copy-start.5
  7.2 0.0 all-gather.2.cloned.1.call-start
  7.2 0.7 all-gather.2.cloned.1.call-update
  7.9 0.0 reduce-scatter.2.cloned.1.call-start
  8.0 0.8 fusion.23
  8.8 0.1 copy.23
  8.9 3.0 %multiply_convert_fusion = bf16[6,256,512]{2,1,0:T(8,128)(2,1)} fusion(bf16[6,256,512]{2,1,0:T(8,128)(2,1)} %param.16, f32[6,256]{1,0:T(8,128)S(1)} %copy.23), kind=kLoop, calls=%fused_computation.21 | loop fusion | flops 2359296 | bytes 3151872 | tf_op jit(solution)/shard_map/convert_element_type | solution.py:20
  11.8 6.0 %collective-permute-start = (bf16[6,256,512]{2,1,0:T(8,128)(2,1)}, bf16[6,256,512]{2,1,0:T(8,128)(2,1)}, u32[]{:S(2)}, u32[]{:S(2)}) collective-permute-start(bf16[6,256,512]{2,1,0:T(8,128)(2,1)} %multiply_convert_fusion), channel_id=1, source_target_pairs={{0,2},{1,3},{2,4},{3,5},{4,6},{5,7},{6,8},{7,9},{8,10},{9,11},{10,... | collective-permute-start | bytes 4718600 | tf_op jit(solution)/shard_map/ppermute | solution.py:10
  17.9 2.6 collective-permute-start.1
  20.5 0.0 copy-done.5
  20.5 0.1 copy.26
  20.6 0.1 reshape.137
  20.7 0.1 copy.25
  20.8 38.1 %collective-permute-done = bf16[6,256,512]{2,1,0:T(8,128)(2,1)} collective-permute-done((bf16[6,256,512]{2,1,0:T(8,128)(2,1)}, bf16[6,256,512]{2,1,0:T(8,128)(2,1)}, u32[]{:S(2)}, u32[]{:S(2)}) %collective-permute-start) | collective-permute-done | bytes 1572896 | tf_op jit(solution)/shard_map/ppermute | solution.py:10
  58.8 0.0 collective-permute-done.1
  58.8 4.1 %pad_maximum_fusion = bf16[18,256,512]{2,1,0:T(8,128)(2,1)} fusion(bf16[6,256,512]{2,1,0:T(8,128)(2,1)} %multiply_convert_fusion, bf16[6,256,512]{2,1,0:T(8,128)(2,1)} %collective-permute-done.1, bf16[6,256,512]{2,1,0:T(8,128)(2,1)} %collective-permute-done), kind=kLoop, calls=%fused_computation.6 | loop fusion | flops 4718592 | bytes 9437184 | tf_op jit(solution)/shard_map/concatenate | solution.py:25
  62.9 6.6 %gather_fusion = bf16[24,256,512]{2,1,0:T(8,128)(2,1)} fusion(bf16[18,256,512]{2,1,0:T(8,128)(2,1)} %pad_maximum_fusion, s32[1024]{0:T(1024)S(1)} %pad_clamp_fusion), kind=kCustom, calls=%fused_computation | custom fusion | bytes 12583008 | tf_op jit(solution)/shard_map/gather | solution.py:30
  69.5 0.0 all-gather.2.cloned.1.call-done
  69.5 8.6 %fusion.10 = f32[6,256,512]{2,1,0:T(8,128)} fusion(bf16[6,256,2048]{2,1,0:T(8,128)(2,1)} %param.20, bf16[2048,512]{1,0:T(8,128)(2,1)} %all-gather.2.cloned.1.call-done), kind=kOutput, calls=%fused_computation.23 | convolution fusion | flops 3221225472 | bytes 11534336 | tf_op jit(solution)/shard_map/dot_general | solution.py:34
  78.1 0.0 copy-done
  78.1 8.7 %multiply_reduce_fusion = (f32[512]{0:T(512)S(1)}, f32[6,512,256]{1,2,0:T(8,128)}) fusion(f32[6,256]{1,0:T(8,128)S(1)} %copy.23, bf16[6,256,256]{2,1,0:T(8,128)(2,1)} %param.22, f32[6,256,512]{2,1,0:T(8,128)} %fusion.10, bf16[6,4,256,256]{3,2,1,0:T(8,128)(2,1)S(1)} %copy-done, bf16[6,4,256,512]{3,2,1,0:T(8,128)(2,1)} %bitcast.52, ...), kind=kOutput, calls=%fused_computation.19 | convolution fusion | flops 2025061888 | bytes 18096152 | tf_op jit(solution)/shard_map/sij,sjt->sit/dot_general | solution.py:42
  86.8 2.8 %fusion.12 = f32[6,512,256]{1,2,0:T(8,128)S(1)} fusion(bf16[6,256,256]{2,1,0:T(8,128)(2,1)} %param.22, f32[6,512,256]{1,2,0:T(8,128)} %get-tuple-element.57, f32[6,256]{1,0:T(8,128)S(1)} %copy.23), kind=kOutput, calls=%fused_computation.25 | convolution fusion | flops 404226048 | bytes 7084032 | tf_op jit(solution)/shard_map/sji,sjt->sit/dot_general | solution.py:46
  89.6 0.0 copy-start.2
  89.6 1.7 copy-done.2
  91.3 8.0 %convolution_bitcast_fusion.1 = f32[2048,512]{0,1:T(8,128)} fusion(bf16[6,256,2048]{2,1,0:T(8,128)(2,1)} %param.20, f32[6,512,256]{1,2,0:T(8,128)S(1)} %fusion.12, f32[6,256]{1,0:T(8,128)S(1)} %copy.23), kind=kOutput, calls=%fused_computation.10 | convolution fusion | flops 3222798336 | bytes 13637632 | tf_op jit(solution)/shard_map/dot_general | solution.py:63
  99.3 0.0 reduce-scatter.2.cloned.1.call-update
  99.3 0.1 copy.29
  99.4 0.1 reshape.133
  99.5 8.4 %convolution_bitcast_fusion = f32[6,4,256,512]{2,3,1,0:T(8,128)} fusion(bf16[6,4,256,256]{3,2,1,0:T(8,128)(2,1)S(1)} %copy-done, f32[6,512,256]{1,2,0:T(8,128)} %copy-done.2, f32[6,256]{1,0:T(8,128)S(1)} %copy.23), kind=kOutput, calls=%fused_computation.7 | convolution fusion | flops 1612185600 | bytes 18880512 | tf_op jit(solution)/shard_map/skij,sit->skjt/dot_general | solution.py:70
  107.9 12.7 %copy.31 = f32[6,4,256,512]{3,2,1,0:T(8,128)} copy(f32[6,4,256,512]{2,3,1,0:T(8,128)} %convolution_bitcast_fusion) | data formatting | bytes 25165824 | tf_op jit(solution)/shard_map/skij,sit->skjt/dot_general | solution.py:70
  120.5 4.8 %broadcast_in_dim.34 = f32[18,256,512]{2,1,0:T(8,128)} broadcast(f32[]{:T(128)} %constant.95.clone.1), dimensions={} | broadcast | bytes 9437188 | tf_op jit(solution)/shard_map/broadcast_in_dim | solution.py:75
  125.3 24.2 %scatter_fusion = f32[18,256,512]{2,1,0:T(8,128)} fusion(f32[18,256,512]{2,1,0:T(8,128)} %broadcast_in_dim.34, s32[24]{0:T(128)S(1)} %fusion.25, f32[24,256,512]{2,1,0:T(8,128)} %bitcast.50), kind=kCustom, calls=%fused_computation.2 | custom fusion | flops 3145728 | bytes 37748832 | tf_op jit(solution)/shard_map/scatter-add | solution.py:77
  149.5 4.9 %convert_element_type.55 = bf16[18,256,512]{2,1,0:T(8,128)(2,1)S(1)} convert(f32[18,256,512]{2,1,0:T(8,128)} %scatter_fusion) | non-fusion elementwise | flops 2359296 | bytes 14155776 | tf_op jit(solution)/shard_map/convert_element_type | solution.py:79
  154.4 0.0 copy-start.3
  154.4 0.0 copy-start.4
  154.4 2.0 fusion.28
  156.4 1.1 copy-done.3
  157.5 1.3 collective-permute-start.2
  158.8 0.0 copy-start.7
  158.8 0.0 copy-start.6
  158.8 1.3 collective-permute-start.3
  160.1 0.0 copy-done.4
  160.1 12.0 %copy.32 = bf16[6,256,256]{0,2,1:T(8,128)(2,1)} copy(bf16[6,256,256]{2,1,0:T(8,128)(2,1)S(1)} %copy-done.4) | data formatting | bytes 1572864 | tf_op args[6]
  172.1 0.0 copy-done.7
  172.1 0.6 reduce_sum.29
  173.4 2.7 gather_fusion.1
  176.1 0.6 fusion.22
  176.7 85.7 %all-reduce = (f32[512]{0:T(512)S(1)}, f32[]{:T(128)}, f32[]{:T(128)}) all-reduce(f32[512]{0:T(512)S(1)} %get-tuple-element.56, f32[]{:T(128)S(6)} %convert_element_type.61, f32[]{:T(128)} %fusion.22), channel_id=1, replica_groups=mesh['parts'=2,'space'=16] {'space'}, use_global_device_ids=true, to_apply=%region_4.5 | all-reduce | flops 514 | bytes 4112 | tf_op jit(solution)/shard_map/psum | solution.py:51
  262.4 0.0 copy-start.1
  262.4 2.2 subtract_divide_fusion
  264.6 0.0 collective-permute-done.2
  264.6 0.0 collective-permute-done.3
  264.6 0.0 copy-done.6
  264.6 5.3 %fusion.6 = bf16[6,256,512]{2,1,0:T(8,128)(2,1)} fusion(bf16[6,256,512]{2,1,0:T(8,128)(2,1)} %collective-permute-done.3, bf16[6,256,512]{2,1,0:T(8,128)(2,1)} %collective-permute-done.2, f32[6,512,256]{1,2,0:T(8,128)} %copy-done.2, bf16[18,256,512]{2,1,0:T(8,128)(2,1)} %copy-done.3, f32[6,256]{1,0:T(8,128)S(1)} %copy.23, f32[512]{0:T(512)S(1)} %copy-done.6, ...), kind=kLoop, calls=%fused_computation.14 | loop fusion | flops 11796480 | bytes 11028480 | tf_op jit(solution)/shard_map/convert_element_type | solution.py:87
  269.9 0.0 reduce-scatter.2.cloned.1.call-done
  269.9 1.8 copy.34
  271.7 0.0 copy-done.1
  (5 shorter events, 0.0 us)
Async XLA Ops:
  7.2 71.0 %copy-start = (bf16[6,4,256,256]{3,2,1,0:T(8,128)(2,1)S(1)}, bf16[6,4,256,256]{3,2,1,0:T(8,128)(2,1)}, u32[]{:S(2)}) copy-start(bf16[6,4,256,256]{3,2,1,0:T(8,128)(2,1)} %param.19) | copy-start | bytes 9437188
  7.2 13.3 %copy-start.5 = (s32[6,4]{0,1:T(4,128)S(1)}, s32[6,4]{0,1:T(4,128)}, u32[]{:S(2)}) copy-start(s32[6,4]{0,1:T(4,128)} %param.18) | copy-start | bytes 292
  7.2 62.4 %all-gather.2.cloned.1.call-start = ((), (), s32[]{:S(2)}) async-start(), calls=%async_computation.1 | async-start | bytes 2228224 | tf_op jit(solution)/shard_map/all_gather | solution.py:36
  7.9 262.0 %reduce-scatter.2.cloned.1.call-start = ((), (), s32[]{:S(2)}) async-start(), calls=%async_computation.2 | async-start | bytes 4456448 | tf_op jit(solution)/shard_map/reduce_scatter | solution.py:62
  11.8 47.0 %collective-permute-start = (bf16[6,256,512]{2,1,0:T(8,128)(2,1)}, bf16[6,256,512]{2,1,0:T(8,128)(2,1)}, u32[]{:S(2)}, u32[]{:S(2)}) collective-permute-start(bf16[6,256,512]{2,1,0:T(8,128)(2,1)} %multiply_convert_fusion), channel_id=1, source_target_pairs={{0,2},{1,3},{2,4},{3,5},{4,6},{5,7},{6,8},{7,9},{8,10},{9,11},{10,... | collective-permute-start | bytes 4718600 | tf_op jit(solution)/shard_map/ppermute | solution.py:10
  17.9 41.0 %collective-permute-start.1 = (bf16[6,256,512]{2,1,0:T(8,128)(2,1)}, bf16[6,256,512]{2,1,0:T(8,128)(2,1)}, u32[]{:S(2)}, u32[]{:S(2)}) collective-permute-start(bf16[6,256,512]{2,1,0:T(8,128)(2,1)} %multiply_convert_fusion), channel_id=1, source_target_pairs={{0,1},{1,2},{2,3},{3,4},{4,5},{5,6},{6,7},{7,8},{8,9},{9,10},{10,1... | collective-permute-start | bytes 4718600 | tf_op jit(solution)/shard_map/ppermute | solution.py:10
  89.6 1.7 copy-start.2
  154.4 3.1 %copy-start.3 = (bf16[18,256,512]{2,1,0:T(8,128)(2,1)}, bf16[18,256,512]{2,1,0:T(8,128)(2,1)S(1)}, u32[]{:S(2)}) copy-start(bf16[18,256,512]{2,1,0:T(8,128)(2,1)S(1)} %convert_element_type.55) | copy-start | bytes 14155780
  154.4 5.7 %copy-start.4 = (bf16[6,256,256]{2,1,0:T(8,128)(2,1)S(1)}, bf16[6,256,256]{2,1,0:T(8,128)(2,1)}, u32[]{:S(2)}) copy-start(bf16[6,256,256]{2,1,0:T(8,128)(2,1)} %param.22) | copy-start | bytes 2359300
  157.5 107.1 %collective-permute-start.2 = (bf16[6,256,512]{2,1,0:T(8,128)(2,1)}, bf16[6,256,512]{2,1,0:T(8,128)(2,1)}, u32[]{:S(2)}, u32[]{:S(2)}) collective-permute-start(bf16[6,256,512]{2,1,0:T(8,128)(2,1)} %get-tuple-element.52), channel_id=1, source_target_pairs={{2,0},{3,1},{4,2},{5,3},{6,4},{7,5},{8,6},{9,7},{10,8},{11,9},{12,... | collective-permute-start | bytes 4718600 | tf_op jit(solution)/shard_map/ppermute | solution.py:10
  158.8 13.3 %copy-start.7 = (s32[6]{0:T(128)S(1)}, s32[6]{0:T(128)}, u32[]{:S(2)}) copy-start(s32[6]{0:T(128)} %param.17) | copy-start | bytes 76
  158.8 105.8 %copy-start.6 = (f32[512]{0:T(512)S(1)}, f32[512]{0:T(512)}, u32[]{:S(2)}) copy-start(f32[512]{0:T(512)} %param.23) | copy-start | bytes 6148
  158.8 105.8 %collective-permute-start.3 = (bf16[6,256,512]{2,1,0:T(8,128)(2,1)}, bf16[6,256,512]{2,1,0:T(8,128)(2,1)}, u32[]{:S(2)}, u32[]{:S(2)}) collective-permute-start(bf16[6,256,512]{2,1,0:T(8,128)(2,1)} %get-tuple-element.53), channel_id=1, source_target_pairs={{1,0},{2,1},{3,2},{4,3},{5,4},{6,5},{7,6},{8,7},{9,8},{10,9},{11,1... | collective-permute-start | bytes 4718600 | tf_op jit(solution)/shard_map/ppermute | solution.py:10
  262.4 9.3 %copy-start.1 = (bf16[6,4,256,256]{3,2,1,0:T(8,128)(2,1)S(1)}, bf16[6,4,256,256]{3,2,1,0:T(8,128)(2,1)}, u32[]{:S(2)}) copy-start(bf16[6,4,256,256]{3,2,1,0:T(8,128)(2,1)} %param.19) | copy-start | bytes 9437188
Sparse Core Ops, SparseCore 0:
  10.2 50.2 all-gather.1
  99.5 99.3 reduce-scatter.1
where the time goes:
time: 279 us
  blocking collectives  85.7 us (31%)
  local copies, waits for them, and re-layouts  45.8 us (16%)
  other arithmetic  45.8 us (16%)
  waiting for transfers between devices  38.8 us (14%)
  matrix products  36.4 us (13%)
  between operations  14.8 us (5%)
  starting transfers between devices  11.3 us (4%)
    psum x1, blocking collectives, local(): lax.psum((jnp.sum(whitened * whitened, axis=(0, 1)), jnp.sum(point_mask *...  85.7 us
    ppermute x4, waiting for transfers between devices, from_behind(): return lax.ppermute(x, axis, pairs)  38.1 us
    scatter-add x1, other arithmetic, local(): window_sums = jnp.zeros((window_length, point_count, field_count), jnp.fl...  24.2 us
    unnamed x18, local copies, waits for them, and re-layouts  16.5 us
    dot_general x1, local copies, waits for them, and re-layouts, local(): jnp.einsum('skij,sit->skjt', krig, adjoint_half, preferred_element_type=j...  12.7 us
    ppermute x4, starting transfers between devices, from_behind(): return lax.ppermute(x, axis, pairs)  11.2 us
    dot_general x1, matrix products, local(): jnp.einsum('sij,sjt->sit', whiten, residual, preferred_element_type=jnp.f...  8.66 us
    dot_general x1, matrix products, local(): jnp.dot(columns, lax.all_gather(knot_values, 'space', axis=0, tiled=True)...  8.58 us
  transfers between devices with their start and end apart: 6, of which 1 were waited for; matrix products, arithmetic and copies ran while one was open for 34% of the time, Pallas kernels for 0%

commit v1 on v0

v1 whole, which is shorter than its diff:
```python
import functools

import jax
import jax.numpy as jnp
from jax import lax
from jax.experimental import pallas as pl
from jax.experimental.pallas import tpu as pltpu
from jax.sharding import PartitionSpec as P

REACH = 9
VMEM_LIMIT = 56 * 1024 * 1024
F32 = jnp.float32
BF16 = jnp.bfloat16


def remote(src, dst, send_sem, recv_sem, target):
    return pltpu.make_async_remote_copy(
        src_ref=src,
        dst_ref=dst,
        send_sem=send_sem,
        recv_sem=recv_sem,
        device_id={"space": target},
        device_id_type=pl.DeviceIdType.MESH,
    )


def flip(i, bit):
    size = 1 << bit
    return i + size - 2 * size * ((i // size) % 2)


def greet(i, n, bits):
    barrier = pltpu.get_barrier_semaphore()
    others = [flip(i, bit) for bit in range(bits)]
    others += [lax.rem(i + by, n) for by in (1, 2, n - 1, n - 2)]
    for other in others:
        pl.semaphore_signal(
            barrier, inc=1, device_id={"space": other}, device_id_type=pl.DeviceIdType.MESH
        )
    pl.semaphore_wait(barrier, len(others))


def row_mask(points, count):
    return (lax.broadcasted_iota(jnp.int32, (points, 1), 0) < count).astype(F32)


def gather_kernel(
    n, bits, counts, obs, load, values, window, base, obs_v, load_v, knots,
    obs_sem, load_sem, near_send, near_recv, far_send, far_recv, pass_send, knot_send, knot_recv,
):
    i = lax.axis_index("space")
    slots, points, fields = obs_v.shape
    far = REACH - slots
    rows = values.shape[0]
    obs_copies = [pltpu.make_async_copy(obs.at[s], obs_v.at[s], obs_sem.at[s]) for s in range(slots)]
    load_copies = [pltpu.make_async_copy(load.at[s], load_v.at[s], load_sem.at[s]) for s in range(slots)]
    for s in reversed(range(slots)):
        obs_copies[s].start()
    for s in range(slots):
        load_copies[s].start()

    def chunk(j):
        return knots.at[pl.ds(pl.multiple_of(j * rows, rows), rows)]

    knots[pl.ds(pl.multiple_of(i * rows, rows), rows), :] = values[...]
    greet(i, n, bits)

    def gather_step(t):
        bit = bits - 1 - t
        stride = 2 << bit
        partner = flip(i, bit)
        sends, receives = [], []
        for m in range(n // stride):
            at = (1 << t) - 1 + m
            mine = chunk(lax.rem(i, stride) + m * stride)
            theirs = chunk(lax.rem(partner, stride) + m * stride)
            sends.append(remote(mine, mine, knot_send.at[at], knot_recv.at[at], partner))
            receives.append(remote(theirs, theirs, knot_send.at[at], knot_recv.at[at], partner))
        return sends, receives

    steps = [gather_step(t) for t in range(bits)]
    for copy in steps[0][0]:
        copy.start()

    def near_copy(s, to):
        return remote(window.at[REACH + s], window.at[far + s], near_send.at[s], near_recv.at[s], to)

    def far_copy(q, to):
        return remote(window.at[REACH + slots - far + q], window.at[q], far_send.at[q], far_recv.at[q], to)

    def pass_copy(q, to):
        return remote(window.at[REACH - far + q], window.at[q], pass_send.at[q], far_recv.at[q], to)

    even = lax.rem(i, 2) == 0
    has_next = i < n - 1
    sends_far = jnp.logical_and(even, i < n - 2)
    passes = jnp.logical_and(even, i > 0)
    next_one, next_two = lax.rem(i + 1, n), lax.rem(i + 2, n)

    for s in reversed(range(slots)):
        obs_copies[s].wait()
        window[REACH + s] = (obs_v[s].astype(F32) * row_mask(points, counts[s])).astype(BF16)

        @pl.when(has_next)
        def _():
            near_copy(s, next_one).start()

        if s >= slots - far:

            @pl.when(sends_far)
            def _():
                far_copy(s - (slots - far), next_two).start()

    for t in range(bits):
        for copy in steps[t][1]:
            copy.wait_recv()
        if t + 1 < bits:
            for copy in steps[t + 1][0]:
                copy.start()

    for q in reversed(range(far)):

        @pl.when(i > 0)
        def _():
            near_copy(slots - far + q, next_one).wait_recv()

        @pl.when(passes)
        def _():
            pass_copy(q, next_one).start()

    for s in range(slots):
        load_copies[s].wait()

    def coarse_step(s, carry):
        coarse = jnp.dot(load_v[s], knots[...], preferred_element_type=F32)
        base[s] = window[REACH + s].astype(F32) - coarse
        return carry

    lax.fori_loop(0, slots, coarse_step, 0)

    @pl.when(i > 0)
    def _():
        for s in range(slots - far):
            near_copy(s, next_one).wait_recv()

    @pl.when(i > 1)
    def _():
        for q in range(far):
            far_copy(q, next_two).wait_recv()

    @pl.when(has_next)
    def _():
        for s in range(slots):
            near_copy(s, next_one).wait_send()

    @pl.when(sends_far)
    def _():
        for q in range(far):
            far_copy(q, next_two).wait_send()

    @pl.when(passes)
    def _():
        for q in range(far):
            pass_copy(q, next_one).wait_send()

    for sends, _ in steps:
        for copy in sends:
            copy.wait_send()


def block_kernel(
    near, counts, window, base, krig, whiten, returned, adjoint_half, rest, stats, sums, adjoints
):
    s = pl.program_id(0)
    slots = pl.num_programs(0)
    neigh, points = krig.shape[1], krig.shape[2]
    window_length = window.shape[0]
    count = counts[s]
    mask = row_mask(points, count)

    @pl.when(s == 0)
    def _():
        sums[...] = jnp.zeros_like(sums)
        stats[...] = jnp.zeros_like(stats)

    predicted = None
    for k in range(neigh):
        at = near[s * neigh + k]
        block = jnp.where(at >= 0, krig[0, k], jnp.zeros((), BF16))
        term = jnp.dot(block, window[jnp.where(at >= 0, at, REACH)], preferred_element_type=F32)
        predicted = term if predicted is None else predicted + term
    factor = whiten[0]
    residual = (mask * (base[0] - predicted)).astype(BF16)
    whitened = mask * jnp.dot(factor, residual, preferred_element_type=F32)
    adjoint = mask * lax.dot_general(
        factor, whitened.astype(BF16), (((0,), (0,)), ((), ())), preferred_element_type=F32
    )
    half = adjoint.astype(BF16)
    adjoint_half[0] = half
    adjoints[s] = adjoint
    diagonal_at = lax.broadcasted_iota(jnp.int32, (points, points), 0) == lax.broadcasted_iota(
        jnp.int32, (points, points), 1
    )
    diagonal = jnp.sum(jnp.where(diagonal_at, factor.astype(F32), 0.0), axis=1, keepdims=True)
    stats[0:1] += jnp.sum(whitened * whitened, axis=0, keepdims=True)
    stats[1:2] += jnp.sum(mask * jnp.log(diagonal), axis=0, keepdims=True)
    stats[2:3] += jnp.full((1, stats.shape[1]), count.astype(F32))
    for k in range(neigh):
        at = near[s * neigh + k]
        to = jnp.where(at >= 0, at, window_length)
        sums[to] += lax.dot_general(
            krig[0, k], half, (((0,), (0,)), ((), ())), preferred_element_type=F32
        )

    @pl.when(s == slots - 1)
    def _():
        def emit(c, carry):
            returned[c] = sums[c].astype(BF16)
            return carry

        def keep(c, carry):
            rest[c] = adjoints[c] - sums[REACH + c].astype(BF16).astype(F32)
            return carry

        lax.fori_loop(0, REACH, emit, 0)
        lax.fori_loop(0, window_length - REACH, keep, 0)


def score_kernel(
    n, bits, counts, noise, stats, half, returned, rest, window, load,
    posterior, loglik, score,
    load_v, rest_v, masked_v, near_v, far_v, partial, landed, stat_v, stat_in,
    local_sem, near_send, near_recv, far_send, far_recv, part_send, part_recv, stat_send, stat_recv,
):
    i = lax.axis_index("space")
    slots, points, fields = rest_v.shape
    far = REACH - slots
    rows = score.shape[0]
    knot_count = partial.shape[0]
    load_copy = pltpu.make_async_copy(load, load_v, local_sem.at[0])
    rest_copy = pltpu.make_async_copy(rest, rest_v, local_sem.at[1])
    masked_copy = pltpu.make_async_copy(window.at[pl.ds(REACH, slots)], masked_v, local_sem.at[2])
    load_copy.start()
    stat_v[0] = stats[...]
    greet(i, n, bits)

    def near_copy(s):
        return remote(
            returned.at[far + s], near_v.at[s], near_send.at[s], near_recv.at[s], lax.rem(i + n - 1, n)
        )

    def far_copy(q):
        return remote(returned.at[q], far_v.at[q], far_send.at[q], far_recv.at[q], lax.rem(i + n - 2, n))

    @pl.when(i > 0)
    def _():
        for s in range(slots):
            near_copy(s).start()

    @pl.when(i > 1)
    def _():
        for q in range(far):
            far_copy(q).start()

    def stat_copy(t):
        return remote(stat_v.at[t], stat_in.at[t], stat_send.at[t], stat_recv.at[t], flip(i, t))

    def piece(j):
        return pl.ds(pl.multiple_of(j * rows, rows), rows)

    def start_of(t):
        return n - (n >> t)

    def part_copy(t, j, m):
        at = start_of(t) + m
        return remote(
            partial.at[piece(j)], landed.at[at], part_send.at[at], part_recv.at[at], flip(i, t)
        )

    stat_copy(0).start()
    load_copy.wait()
    rest_copy.start()
    masked_copy.start()

    tile = min(256, knot_count)
    pairs = tile // rows // 2
    other = 1 - lax.rem(i, 2)

    def tile_step(u, carry):
        at = pl.multiple_of(u * tile, tile)
        partial[pl.ds(at, tile), :] = lax.dot_general(
            load_v[:, pl.ds(at, tile)], half[...], (((0,), (0,)), ((), ())), preferred_element_type=F32
        )
        for q in range(pairs):
            m = u * pairs + q
            part_copy(0, 2 * m + other, m).start()
        return carry

    lax.fori_loop(0, knot_count // tile, tile_step, 0)

    def settle(j, steps):
        for t in range(steps):
            m = j // (2 << t)
            at = start_of(t) + m
            part_copy(t, j, m).wait_recv()
            partial[piece(j), :] += landed[at]

    for t in range(1, bits + 1):
        stat_copy(t - 1).wait_recv()
        stat_v[t] = stat_v[t - 1] + stat_in[t - 1]
        if t < bits:
            stat_copy(t).start()
            low = lax.rem(flip(i, t), 2 << t)
            for m in range(n >> (t + 1)):
                j = low + m * (2 << t)
                settle(j, t)
                part_copy(t, j, m).start()
    settle(i, bits)
    score[...] = partial[piece(i), :]
    totals = stat_v[bits]
    loglik[...] = (totals[1:2] - 0.5 * totals[0:1]) / totals[2:3]

    rest_copy.wait()
    masked_copy.wait()
    for s in reversed(range(slots)):

        @pl.when(i < n - 1)
        def _():
            near_copy(s).wait_recv()
            rest_v[s] = rest_v[s] - near_v[s].astype(F32)

        if s >= slots - far:

            @pl.when(i < n - 2)
            def _():
                far_copy(s - (slots - far)).wait_recv()
                rest_v[s] = rest_v[s] - far_v[s - (slots - far)].astype(F32)

        precision = row_mask(points, counts[s]) * rest_v[s]
        posterior[s] = (masked_v[s].astype(F32) - noise[...] * precision).astype(BF16)

    @pl.when(i > 0)
    def _():
        for s in range(slots):
            near_copy(s).wait_send()

    @pl.when(i > 1)
    def _():
        for q in range(far):
            far_copy(q).wait_send()

    for t in range(bits):
        stat_copy(t).wait_send()
        low = lax.rem(flip(i, t), 2 << t)
        for m in range(n >> (t + 1)):
            part_copy(t, low + m * (2 << t), m).wait_send()


def vmem():
    return pl.BlockSpec(memory_space=pltpu.VMEM)


def smem():
    return pl.BlockSpec(memory_space=pltpu.SMEM)


def anywhere():
    return pl.BlockSpec(memory_space=pl.ANY)


def local(n, obs, counts, neighbours, krig, knot_load, knot_values, whiten, noise_var):
    bits = n.bit_length() - 1
    slots, points, fields = obs.shape
    knot_count = knot_load.shape[2]
    neigh = neighbours.shape[1]
    far = REACH - slots
    window_length = REACH + slots
    rows = knot_values.shape[0]
    dma = pltpu.SemaphoreType.DMA

    window, base = pl.pallas_call(
        functools.partial(gather_kernel, n, bits),
        out_shape=(
            jax.ShapeDtypeStruct((window_length, points, fields), BF16),
            jax.ShapeDtypeStruct((slots, points, fields), F32),
        ),
        in_specs=[smem(), anywhere(), anywhere(), vmem()],
        out_specs=(vmem(), vmem()),
        scratch_shapes=[
            pltpu.VMEM((slots, points, fields), BF16),
            pltpu.VMEM((slots, points, knot_count), BF16),
            pltpu.VMEM((knot_count, fields), BF16),
            dma((slots,)), dma((slots,)), dma((slots,)), dma((slots,)),
            dma((far,)), dma((far,)), dma((far,)), dma((n - 1,)), dma((n - 1,)),
        ],
        compiler_params=pltpu.CompilerParams(
            collective_id=0, has_side_effects=True, vmem_limit_bytes=VMEM_LIMIT
        ),
    )(counts, obs, knot_load, knot_values)

    anchor = lax.axis_index("space") * slots - REACH
    near = jnp.where(neighbours >= 0, neighbours - anchor, -1).reshape(-1)

    def whole(*shape):
        return pl.BlockSpec(shape, lambda s, *_: (0,) * len(shape))

    def slot(*shape):
        return pl.BlockSpec((1,) + shape, lambda s, *_: (s,) + (0,) * len(shape))

    returned, adjoint_half, rest, stats = pl.pallas_call(
        block_kernel,
        out_shape=(
            jax.ShapeDtypeStruct((REACH, points, fields), BF16),
            jax.ShapeDtypeStruct((slots, points, fields), BF16),
            jax.ShapeDtypeStruct((slots, points, fields), F32),
            jax.ShapeDtypeStruct((8, fields), F32),
        ),
        grid_spec=pltpu.PrefetchScalarGridSpec(
            num_scalar_prefetch=2,
            grid=(slots,),
            in_specs=[
                whole(window_length, points, fields),
                slot(points, fields),
                slot(neigh, points, points),
                slot(points, points),
            ],
            out_specs=(
                whole(REACH, points, fields),
                slot(points, fields),
                whole(slots, points, fields),
                whole(8, fields),
            ),
            scratch_shapes=[
                pltpu.VMEM((window_length + 1, points, fields), F32),
                pltpu.VMEM((slots, points, fields), F32),
            ],
        ),
        compiler_params=pltpu.CompilerParams(
            dimension_semantics=("arbitrary",), vmem_limit_bytes=VMEM_LIMIT
        ),
    )(near, counts, window, base, krig, whiten)

    posterior, loglik, score = pl.pallas_call(
        functools.partial(score_kernel, n, bits),
        out_shape=(
            jax.ShapeDtypeStruct((slots, points, fields), BF16),
            jax.ShapeDtypeStruct((1, fields), F32),
            jax.ShapeDtypeStruct((rows, fields), F32),
        ),
        in_specs=[smem(), vmem(), vmem(), vmem(), anywhere(), anywhere(), anywhere(), anywhere()],
        out_specs=(vmem(), vmem(), vmem()),
        scratch_shapes=[
            pltpu.VMEM((slots * points, knot_count), BF16),
            pltpu.VMEM((slots, points, fields), F32),
            pltpu.VMEM((slots, points, fields), BF16),
            pltpu.VMEM((slots, points, fields), BF16),
            pltpu.VMEM((far, points, fields), BF16),
            pltpu.VMEM((knot_count, fields), F32),
            pltpu.VMEM((n - 1, rows, fields), F32),
            pltpu.VMEM((bits + 1, 8, fields), F32),
            pltpu.VMEM((bits, 8, fields), F32),
            dma((3,)), dma((slots,)), dma((slots,)), dma((far,)), dma((far,)),
            dma((n - 1,)), dma((n - 1,)), dma((bits,)), dma((bits,)),
        ],
        compiler_params=pltpu.CompilerParams(
            collective_id=1, has_side_effects=True, vmem_limit_bytes=VMEM_LIMIT
        ),
    )(
        counts,
        noise_var[None, :],
        stats,
        adjoint_half.reshape(slots * points, fields),
        returned,
        rest,
        window,
        knot_load.reshape(slots * points, knot_count),
    )
    return posterior, loglik.reshape(fields), score


def solution(mesh):
    in_specs = (
        P(("parts", "space"), None, None),
        P(("parts", "space")),
        P(("parts", "space"), None),
        P(("parts", "space"), None, None, None),
        P(("parts", "space"), None, None),
        P(("parts", "space"), None),
        P(("parts", "space"), None, None),
        P(),
    )
    out_specs = (P(("parts", "space"), None, None), P("parts"), P(("parts", "space"), None))
    return jax.shard_map(
        functools.partial(local, mesh.shape["space"]),
        mesh=mesh,
        in_specs=in_specs,
        out_specs=out_specs,
        check_vma=False,
    )
```

time: 279 us -> 161 us (0.58)
  the two profiles are of different devices: /device:TPU:0 before, /device:TPU:30 now
where the time goes in v1:
time: 161 us
  Pallas kernels  154 us (96%)
  local copies, waits for them, and re-layouts  4.75 us (3%)
    pallas_call x1, Pallas kernels, local(): pl.pallas_call(functools.partial(score_kernel, n, bits), out_shape=(jax.S...  89.2 us
    pallas_call x1, Pallas kernels, local(): pl.pallas_call(functools.partial(gather_kernel, n, bits), out_shape=(jax....  50.3 us
    pallas_call x1, Pallas kernels, local(): pl.pallas_call(block_kernel, out_shape=(jax.ShapeDtypeStruct((REACH, poin...  14.9 us
    unnamed x7, local copies, waits for them, and re-layouts  4.07 us

profile of v1, /device:TPU:30, one launch (start us, length us, event | category | flops | bytes accessed | tf_op | source)
XLA Modules:
  0.0 160.6 jit_solution(12010809696147349353)
XLA Ops:
  0.6 0.7 subtract_select_fusion
  1.3 0.1 copy.12
  1.4 0.6 reshape.18.near
  2.0 50.3 %shard_map.103 = (bf16[15,256,512]{2,1,0:T(8,128)(2,1)}, f32[6,256,512]{2,1,0:T(8,128)}) custom-call(s32[6]{0:T(128)} %counts.5, bf16[6,256,512]{2,1,0:T(8,128)(2,1)} %obs.1, bf16[6,256,2048]{2,1,0:T(8,128)(2,1)} %load.1, bf16[128,512]{1,0:T(8,128)(2,1)} %values.1), custom_call_target="tpu_custom_call" | custom-call | tf_op jit(solution)/shard_map/pallas_call | solution.py:381
  52.3 14.9 %shard_map.104 = (bf16[9,256,512]{2,1,0:T(8,128)(2,1)}, bf16[6,256,512]{2,1,0:T(8,128)(2,1)}, f32[6,256,512]{2,1,0:T(8,128)}, f32[8,512]{1,0:T(8,128)}) custom-call(s32[24]{0:T(128)} %reshape.18.near, s32[6]{0:T(128)} %counts.5, bf16[15,256,512]{2,1,0:T(8,128)(2,1)} %get-tuple-element.12.window, f32[6,256,512]{2,1,0:T(8,128)} %get-tuple-element.13.base, ...), custom_call_target="tpu_custom_call" | custom-call | tf_op jit(solution)/shard_map/pallas_call | solution.py:410
  67.3 89.2 %shard_map.105 = (bf16[6,256,512]{2,1,0:T(8,128)(2,1)}, f32[1,512]{1,0:T(1,128)}, f32[128,512]{1,0:T(8,128)}) custom-call(s32[6]{0:T(128)} %counts.5, f32[1,512]{1,0:T(1,128)} %bitcast.6, f32[8,512]{1,0:T(8,128)} %get-tuple-element.14.stats, bf16[1536,512]{1,0:T(8,128)(2,1)} %bitcast.5, bf16[9,256,512]{2,1,0:T(8,128)(2,1)} %get-tuple-element.16.returned, ...), custom_call_target="tpu_custom_call" | custom-call | tf_op jit(solution)/shard_map/pallas_call | solution.py:443
  156.5 0.0 copy-start.1
  156.5 0.0 copy-start
  156.5 2.8 %copy.16 = bf16[6,256,512]{2,1,0:T(8,128)(2,1)} copy(bf16[6,256,512]{2,1,0:T(8,128)(2,1)} %get-tuple-element.24) | data formatting | bytes 3145728
  159.3 0.0 copy-done.1
  159.3 0.6 copy.17
  159.9 0.0 copy-done
  159.9 0.7 copy.18
Async XLA Ops:
  156.5 2.8 %copy-start.1 = (f32[1,512]{1,0:T(1,128)S(1)}, f32[1,512]{1,0:T(1,128)}, u32[]{:S(2)}) copy-start(f32[1,512]{1,0:T(1,128)} %get-tuple-element.19) | copy-start | bytes 6148
  156.5 3.4 %copy-start = (f32[128,512]{1,0:T(8,128)S(1)}, f32[128,512]{1,0:T(8,128)}, u32[]{:S(2)}) copy-start(f32[128,512]{1,0:T(8,128)} %get-tuple-element.26) | copy-start | bytes 786436

commit v2 on v1

--- a/solution.py
+++ b/solution.py
@@ -101,15 +101,11 @@
         obs_copies[s].wait()
         window[REACH + s] = (obs_v[s].astype(F32) * row_mask(points, counts[s])).astype(BF16)
 
-        @pl.when(has_next)
-        def _():
-            near_copy(s, next_one).start()
-
         if s >= slots - far:
 
-            @pl.when(sends_far)
+            @pl.when(has_next)
             def _():
-                far_copy(s - (slots - far), next_two).start()
+                near_copy(s, next_one).start()
 
     for t in range(bits):
         for copy in steps[t][1]:
@@ -117,6 +113,17 @@
         if t + 1 < bits:
             for copy in steps[t + 1][0]:
                 copy.start()
+        if t == bits - 2:
+
+            @pl.when(sends_far)
+            def _():
+                for q in reversed(range(far)):
+                    far_copy(q, next_two).start()
+
+            @pl.when(has_next)
+            def _():
+                for s in reversed(range(slots - far)):
+                    near_copy(s, next_one).start()
 
     for q in reversed(range(far)):
 
@@ -171,48 +178,65 @@
 def block_kernel(
     near, counts, window, base, krig, whiten, returned, adjoint_half, rest, stats, sums, adjoints
 ):
-    s = pl.program_id(0)
-    slots = pl.num_programs(0)
-    neigh, points = krig.shape[1], krig.shape[2]
+    step = pl.program_id(0)
+    group, neigh, points = krig.shape[0], krig.shape[1], krig.shape[2]
     window_length = window.shape[0]
-    count = counts[s]
-    mask = row_mask(points, count)
-
-    @pl.when(s == 0)
+    slots = window_length - REACH
+    anchor = lax.axis_index("space") * slots - REACH
+    members = range(group)
+    ids = [step * group + g for g in members]
+    masks = [row_mask(points, counts[s]) for s in ids]
+
+    @pl.when(step == 0)
     def _():
         sums[...] = jnp.zeros_like(sums)
         stats[...] = jnp.zeros_like(stats)
 
-    predicted = None
-    for k in range(neigh):
-        at = near[s * neigh + k]
-        block = jnp.where(at >= 0, krig[0, k], jnp.zeros((), BF16))
-        term = jnp.dot(block, window[jnp.where(at >= 0, at, REACH)], preferred_element_type=F32)
-        predicted = term if predicted is None else predicted + term
-    factor = whiten[0]
-    residual = (mask * (base[0] - predicted)).astype(BF16)
-    whitened = mask * jnp.dot(factor, residual, preferred_element_type=F32)
-    adjoint = mask * lax.dot_general(
-        factor, whitened.astype(BF16), (((0,), (0,)), ((), ())), preferred_element_type=F32
-    )
-    half = adjoint.astype(BF16)
-    adjoint_half[0] = half
-    adjoints[s] = adjoint
+    places = [[near[s, k] - anchor for k in range(neigh)] for s in ids]
+    valid = [[near[s, k] >= 0 for k in range(neigh)] for s in ids]
+    predicted = []
+    for g in members:
+        total = None
+        for k in range(neigh):
+            block = jnp.where(valid[g][k], krig[g, k], jnp.zeros((), BF16))
+            rows = window[jnp.where(valid[g][k], places[g][k], REACH)]
+            term = jnp.dot(block, rows, preferred_element_type=F32)
+            total = term if total is None else total + term
+        predicted.append(total)
+    residual = [(masks[g] * (base[g] - predicted[g])).astype(BF16) for g in members]
+    whitened = [
+        masks[g] * jnp.dot(whiten[g], residual[g], preferred_element_type=F32) for g in members
+    ]
+    whitened_half = [w.astype(BF16) for w in whitened]
+    adjoint = [
+        masks[g]
+        * lax.dot_general(
+            whiten[g], whitened_half[g], (((0,), (0,)), ((), ())), preferred_element_type=F32
+        )
+        for g in members
+    ]
+    half = [a.astype(BF16) for a in adjoint]
+    for g in members:
+        adjoint_half[g] = half[g]
+        adjoints[ids[g]] = adjoint[g]
+    for g in members:
+        for k in range(neigh):
+            to = jnp.where(valid[g][k], places[g][k], window_length)
+            sums[to] += lax.dot_general(
+                krig[g, k], half[g], (((0,), (0,)), ((), ())), preferred_element_type=F32
+            )
     diagonal_at = lax.broadcasted_iota(jnp.int32, (points, points), 0) == lax.broadcasted_iota(
         jnp.int32, (points, points), 1
     )
-    diagonal = jnp.sum(jnp.where(diagonal_at, factor.astype(F32), 0.0), axis=1, keepdims=True)
-    stats[0:1] += jnp.sum(whitened * whitened, axis=0, keepdims=True)
-    stats[1:2] += jnp.sum(mask * jnp.log(diagonal), axis=0, keepdims=True)
-    stats[2:3] += jnp.full((1, stats.shape[1]), count.astype(F32))
-    for k in range(neigh):
-        at = near[s * neigh + k]
-        to = jnp.where(at >= 0, at, window_length)
-        sums[to] += lax.dot_general(
-            krig[0, k], half, (((0,), (0,)), ((), ())), preferred_element_type=F32
+    for g in members:
+        diagonal = jnp.sum(
+            jnp.where(diagonal_at, whiten[g].astype(F32), 0.0), axis=1, keepdims=True
         )
-
-    @pl.when(s == slots - 1)
+        stats[0:1] += jnp.sum(whitened[g] * whitened[g], axis=0, keepdims=True)
+        stats[1:2] += jnp.sum(masks[g] * jnp.log(diagonal), axis=0, keepdims=True)
+        stats[2:3] += jnp.full((1, stats.shape[1]), counts[ids[g]].astype(F32))
+
+    @pl.when(step == pl.num_programs(0) - 1)
     def _():
         def emit(c, carry):
             returned[c] = sums[c].astype(BF16)
@@ -223,7 +247,7 @@
             return carry
 
         lax.fori_loop(0, REACH, emit, 0)
-        lax.fori_loop(0, window_length - REACH, keep, 0)
+        lax.fori_loop(0, slots, keep, 0)
 
 
 def score_kernel(
@@ -252,11 +276,6 @@
     def far_copy(q):
         return remote(returned.at[q], far_v.at[q], far_send.at[q], far_recv.at[q], lax.rem(i + n - 2, n))
 
-    @pl.when(i > 0)
-    def _():
-        for s in range(slots):
-            near_copy(s).start()
-
     @pl.when(i > 1)
     def _():
         for q in range(far):
@@ -315,6 +334,13 @@
                 j = low + m * (2 << t)
                 settle(j, t)
                 part_copy(t, j, m).start()
+        if t == 2:
+
+            @pl.when(i > 0)
+            def _():
+                for s in reversed(range(slots)):
+                    near_copy(s).start()
+
     settle(i, bits)
     score[...] = partial[piece(i), :]
     totals = stat_v[bits]
@@ -398,14 +424,13 @@
         ),
     )(counts, obs, knot_load, knot_values)
 
-    anchor = lax.axis_index("space") * slots - REACH
-    near = jnp.where(neighbours >= 0, neighbours - anchor, -1).reshape(-1)
+    group = 2 - slots % 2
 
     def whole(*shape):
         return pl.BlockSpec(shape, lambda s, *_: (0,) * len(shape))
 
     def slot(*shape):
-        return pl.BlockSpec((1,) + shape, lambda s, *_: (s,) + (0,) * len(shape))
+        return pl.BlockSpec((group,) + shape, lambda s, *_: (s,) + (0,) * len(shape))
 
     returned, adjoint_half, rest, stats = pl.pallas_call(
         block_kernel,
@@ -417,7 +442,7 @@
         ),
         grid_spec=pltpu.PrefetchScalarGridSpec(
             num_scalar_prefetch=2,
-            grid=(slots,),
+            grid=(slots // group,),
             in_specs=[
                 whole(window_length, points, fields),
                 slot(points, fields),
@@ -438,7 +463,7 @@
         compiler_params=pltpu.CompilerParams(
             dimension_semantics=("arbitrary",), vmem_limit_bytes=VMEM_LIMIT
         ),
-    )(near, counts, window, base, krig, whiten)
+    )(neighbours, counts, window, base, krig, whiten)
 
     posterior, loglik, score = pl.pallas_call(
         functools.partial(score_kernel, n, bits),

time: 161 us -> 173 us (1.075)
  the two profiles are of different devices: /device:TPU:30 before, /device:TPU:17 now
where the time goes in v2:
time: 173 us
  Pallas kernels  167 us (97%)
  local copies, waits for them, and re-layouts  5.43 us (3%)
    pallas_call x1, Pallas kernels, local(): pl.pallas_call(functools.partial(score_kernel, n, bits), out_shape=(jax.S...  95.1 us
    pallas_call x1, Pallas kernels, local(): pl.pallas_call(functools.partial(gather_kernel, n, bits), out_shape=(jax....  58.3 us
    pallas_call x1, Pallas kernels, local(): pl.pallas_call(block_kernel, out_shape=(jax.ShapeDtypeStruct((REACH, poin...  13.2 us
    unnamed x8, local copies, waits for them, and re-layouts  5.43 us

profile of v2, /device:TPU:17, one launch (start us, length us, event | category | flops | bytes accessed | tf_op | source)
XLA Modules:
  0.0 172.8 jit_solution(7119889403371237248)
XLA Ops:
  0.6 1.4 copy.11.near
  2.0 58.3 %shard_map.103 = (bf16[15,256,512]{2,1,0:T(8,128)(2,1)}, f32[6,256,512]{2,1,0:T(8,128)}) custom-call(s32[6]{0:T(128)} %counts.5, bf16[6,256,512]{2,1,0:T(8,128)(2,1)} %obs.1, bf16[6,256,2048]{2,1,0:T(8,128)(2,1)} %load.1, bf16[128,512]{1,0:T(8,128)(2,1)} %values.1), custom_call_target="tpu_custom_call" | custom-call | tf_op jit(solution)/shard_map/pallas_call | solution.py:407
  60.3 13.2 %shard_map.104 = (bf16[9,256,512]{2,1,0:T(8,128)(2,1)}, bf16[6,256,512]{2,1,0:T(8,128)(2,1)}, f32[6,256,512]{2,1,0:T(8,128)}, f32[8,512]{1,0:T(8,128)}) custom-call(s32[6,4]{1,0:T(8,128)} %copy.11.near, s32[6]{0:T(128)} %counts.5, bf16[15,256,512]{2,1,0:T(8,128)(2,1)} %get-tuple-element.12.window, f32[6,256,512]{2,1,0:T(8,128)} %get-tuple-element.13.base, ...), custom_call_target="tpu_custom_call" | custom-call | tf_op jit(solution)/shard_map/pallas_call | solution.py:435
  73.5 95.1 %shard_map.105 = (bf16[6,256,512]{2,1,0:T(8,128)(2,1)}, f32[1,512]{1,0:T(1,128)}, f32[128,512]{1,0:T(8,128)}) custom-call(s32[6]{0:T(128)} %counts.5, f32[1,512]{1,0:T(1,128)} %bitcast.6, f32[8,512]{1,0:T(8,128)} %get-tuple-element.14.stats, bf16[1536,512]{1,0:T(8,128)(2,1)} %bitcast.5, bf16[9,256,512]{2,1,0:T(8,128)(2,1)} %get-tuple-element.16.returned, ...), custom_call_target="tpu_custom_call" | custom-call | tf_op jit(solution)/shard_map/pallas_call | solution.py:468
  168.7 0.0 copy-start.1
  168.7 0.0 copy-start
  168.7 2.8 %copy.15 = bf16[6,256,512]{2,1,0:T(8,128)(2,1)} copy(bf16[6,256,512]{2,1,0:T(8,128)(2,1)} %get-tuple-element.24) | data formatting | bytes 3145728
  171.5 0.0 copy-done.1
  171.5 0.6 copy.16
  172.1 0.0 copy-done
  172.1 0.7 copy.17
Async XLA Ops:
  168.7 2.8 %copy-start.1 = (f32[1,512]{1,0:T(1,128)S(1)}, f32[1,512]{1,0:T(1,128)}, u32[]{:S(2)}) copy-start(f32[1,512]{1,0:T(1,128)} %get-tuple-element.19) | copy-start | bytes 6148
  168.7 3.4 %copy-start = (f32[128,512]{1,0:T(8,128)S(1)}, f32[128,512]{1,0:T(8,128)}, u32[]{:S(2)}) copy-start(f32[128,512]{1,0:T(8,128)} %get-tuple-element.26) | copy-start | bytes 786436

commit v3 on v2

--- a/solution.py
+++ b/solution.py
@@ -65,22 +65,36 @@
     knots[pl.ds(pl.multiple_of(i * rows, rows), rows), :] = values[...]
     greet(i, n, bits)
 
-    def gather_step(t):
+    def exchange(first, count, stride, mine, partner, theirs):
+        sends, receives = [], []
+        for m in range(count):
+            at = first + m
+            out, back = chunk(mine + m * stride), chunk(theirs + m * stride)
+            sends.append(remote(out, out, knot_send.at[at], knot_recv.at[at], partner))
+            receives.append(remote(back, back, knot_send.at[at], knot_recv.at[at], partner))
+        return sends, receives
+
+    def line_step(t):
         bit = bits - 1 - t
         stride = 2 << bit
         partner = flip(i, bit)
-        sends, receives = [], []
-        for m in range(n // stride):
-            at = (1 << t) - 1 + m
-            mine = chunk(lax.rem(i, stride) + m * stride)
-            theirs = chunk(lax.rem(partner, stride) + m * stride)
-            sends.append(remote(mine, mine, knot_send.at[at], knot_recv.at[at], partner))
-            receives.append(remote(theirs, theirs, knot_send.at[at], knot_recv.at[at], partner))
-        return sends, receives
-
-    steps = [gather_step(t) for t in range(bits)]
-    for copy in steps[0][0]:
-        copy.start()
+        return exchange(
+            (1 << t) - 1, n // stride, stride, lax.rem(i, stride), partner, lax.rem(partner, stride)
+        )
+
+    def start(copies):
+        for copy in copies:
+            copy.start()
+
+    lines = bits - 2
+    held = n // 4
+    steps = [line_step(t) for t in range(lines)]
+    pair, side = flip(i, 0), flip(i, 1)
+    mine, pair_low, side_low = lax.rem(i, 4), lax.rem(pair, 4), lax.rem(side, 4)
+    over_pair = exchange(held - 1, held, 4, mine, pair, pair_low)
+    over_side = exchange(2 * held - 1, held, 4, mine, side, side_low)
+    relay = exchange(3 * held - 1, held, 4, side_low, pair, flip(side_low, 0))
+    start(steps[0][0])
 
     def near_copy(s, to):
         return remote(window.at[REACH + s], window.at[far + s], near_send.at[s], near_recv.at[s], to)
@@ -101,29 +115,47 @@
         obs_copies[s].wait()
         window[REACH + s] = (obs_v[s].astype(F32) * row_mask(points, counts[s])).astype(BF16)
 
+        @pl.when(has_next)
+        def _():
+            near_copy(s, next_one).start()
+
         if s >= slots - far:
 
-            @pl.when(has_next)
+            @pl.when(sends_far)
             def _():
-                near_copy(s, next_one).start()
-
-    for t in range(bits):
+                far_copy(s - (slots - far), next_two).start()
+
+    for t in range(lines):
         for copy in steps[t][1]:
             copy.wait_recv()
-        if t + 1 < bits:
-            for copy in steps[t + 1][0]:
-                copy.start()
-        if t == bits - 2:
-
-            @pl.when(sends_far)
-            def _():
-                for q in reversed(range(far)):
-                    far_copy(q, next_two).start()
-
-            @pl.when(has_next)
-            def _():
-                for s in reversed(range(slots - far)):
-                    near_copy(s, next_one).start()
+        start(steps[t + 1][0] if t + 1 < lines else over_side[0] + over_pair[0])
+
+    width = 2 * rows
+    staged = width % 128 == 0
+
+    def coarse_part(s, low):
+        total = None
+        for m in range(held):
+            at = pl.ds(pl.multiple_of((low + 4 * m) * rows, width), width)
+            term = jnp.dot(load_v[s, :, at], knots[at, :], preferred_element_type=F32)
+            total = term if total is None else total + term
+        return total
+
+    for s in range(slots):
+        load_copies[s].wait()
+    for copy in over_pair[1]:
+        copy.wait_recv()
+    if staged:
+
+        def first_step(s, carry):
+            base[s] = window[REACH + s].astype(F32) - coarse_part(s, mine - lax.rem(mine, 2))
+            return carry
+
+        lax.fori_loop(0, slots, first_step, 0)
+
+    for arrive, onward in zip(over_side[1], relay[0]):
+        arrive.wait_recv()
+        onward.start()
 
     for q in reversed(range(far)):
 
@@ -135,15 +167,18 @@
         def _():
             pass_copy(q, next_one).start()
 
-    for s in range(slots):
-        load_copies[s].wait()
-
-    def coarse_step(s, carry):
-        coarse = jnp.dot(load_v[s], knots[...], preferred_element_type=F32)
-        base[s] = window[REACH + s].astype(F32) - coarse
+    for copy in relay[1]:
+        copy.wait_recv()
+
+    def last_step(s, carry):
+        if staged:
+            base[s] -= coarse_part(s, side_low - lax.rem(side_low, 2))
+        else:
+            coarse = jnp.dot(load_v[s], knots[...], preferred_element_type=F32)
+            base[s] = window[REACH + s].astype(F32) - coarse
         return carry
 
-    lax.fori_loop(0, slots, coarse_step, 0)
+    lax.fori_loop(0, slots, last_step, 0)
 
     @pl.when(i > 0)
     def _():
@@ -170,7 +205,7 @@
         for q in range(far):
             pass_copy(q, next_one).wait_send()
 
-    for sends, _ in steps:
+    for sends, _ in steps + [over_pair, over_side, relay]:
         for copy in sends:
             copy.wait_send()
 
@@ -251,9 +286,9 @@
 
 
 def score_kernel(
-    n, bits, counts, noise, stats, half, returned, rest, window, load,
-    posterior, loglik, score,
-    load_v, rest_v, masked_v, near_v, far_v, partial, landed, stat_v, stat_in,
+    n, bits, stats, half, returned, rest, load,
+    rest_v, totals, score,
+    load_v, near_v, far_v, partial, landed, stat_v, stat_in,
     local_sem, near_send, near_recv, far_send, far_recv, part_send, part_recv, stat_send, stat_recv,
 ):
     i = lax.axis_index("space")
@@ -263,7 +298,6 @@
     knot_count = partial.shape[0]
     load_copy = pltpu.make_async_copy(load, load_v, local_sem.at[0])
     rest_copy = pltpu.make_async_copy(rest, rest_v, local_sem.at[1])
-    masked_copy = pltpu.make_async_copy(window.at[pl.ds(REACH, slots)], masked_v, local_sem.at[2])
     load_copy.start()
     stat_v[0] = stats[...]
     greet(i, n, bits)
@@ -299,7 +333,6 @@
     stat_copy(0).start()
     load_copy.wait()
     rest_copy.start()
-    masked_copy.start()
 
     tile = min(256, knot_count)
     pairs = tile // rows // 2
@@ -343,11 +376,9 @@
 
     settle(i, bits)
     score[...] = partial[piece(i), :]
-    totals = stat_v[bits]
-    loglik[...] = (totals[1:2] - 0.5 * totals[0:1]) / totals[2:3]
+    totals[...] = stat_v[bits]
 
     rest_copy.wait()
-    masked_copy.wait()
     for s in reversed(range(slots)):
 
         @pl.when(i < n - 1)
@@ -361,9 +392,6 @@
             def _():
                 far_copy(s - (slots - far)).wait_recv()
                 rest_v[s] = rest_v[s] - far_v[s - (slots - far)].astype(F32)
-
-        precision = row_mask(points, counts[s]) * rest_v[s]
-        posterior[s] = (masked_v[s].astype(F32) - noise[...] * precision).astype(BF16)
 
     @pl.when(i > 0)
     def _():
@@ -465,42 +493,42 @@
         ),
     )(neighbours, counts, window, base, krig, whiten)
 
-    posterior, loglik, score = pl.pallas_call(
+    rest, totals, score = pl.pallas_call(
         functools.partial(score_kernel, n, bits),
         out_shape=(
-            jax.ShapeDtypeStruct((slots, points, fields), BF16),
-            jax.ShapeDtypeStruct((1, fields), F32),
+            jax.ShapeDtypeStruct((slots, points, fields), F32),
+            jax.ShapeDtypeStruct((8, fields), F32),
             jax.ShapeDtypeStruct((rows, fields), F32),
         ),
-        in_specs=[smem(), vmem(), vmem(), vmem(), anywhere(), anywhere(), anywhere(), anywhere()],
+        in_specs=[vmem(), vmem(), anywhere(), anywhere(), anywhere()],
         out_specs=(vmem(), vmem(), vmem()),
         scratch_shapes=[
             pltpu.VMEM((slots * points, knot_count), BF16),
-            pltpu.VMEM((slots, points, fields), F32),
-            pltpu.VMEM((slots, points, fields), BF16),
             pltpu.VMEM((slots, points, fields), BF16),
             pltpu.VMEM((far, points, fields), BF16),
             pltpu.VMEM((knot_count, fields), F32),
             pltpu.VMEM((n - 1, rows, fields), F32),
             pltpu.VMEM((bits + 1, 8, fields), F32),
             pltpu.VMEM((bits, 8, fields), F32),
-            dma((3,)), dma((slots,)), dma((slots,)), dma((far,)), dma((far,)),
+            dma((2,)), dma((slots,)), dma((slots,)), dma((far,)), dma((far,)),
             dma((n - 1,)), dma((n - 1,)), dma((bits,)), dma((bits,)),
         ],
         compiler_params=pltpu.CompilerParams(
             collective_id=1, has_side_effects=True, vmem_limit_bytes=VMEM_LIMIT
         ),
     )(
-        counts,
-        noise_var[None, :],
         stats,
         adjoint_half.reshape(slots * points, fields),
         returned,
         rest,
-        window,
         knot_load.reshape(slots * points, knot_count),
     )
-    return posterior, loglik.reshape(fields), score
+    valid = jnp.arange(points)[None, :, None] < counts[:, None, None]
+    precision = jnp.where(valid, rest, 0.0)
+    masked = jnp.where(valid, obs.astype(F32), 0.0)
+    posterior = (masked - noise_var[None, None, :] * precision).astype(BF16)
+    loglik = (totals[1] - 0.5 * totals[0]) / totals[2]
+    return posterior, loglik, score
 
 
 def solution(mesh):

time: 173 us -> 153 us (0.88)
  the two profiles are of different devices: /device:TPU:17 before, /device:TPU:0 now
where the time goes in v3:
time: 153 us; the launch traced here: 152 us
  Pallas kernels  146 us (95%)
  other arithmetic  4.67 us (3%)
    pallas_call x1, Pallas kernels, local(): pl.pallas_call(functools.partial(score_kernel, n, bits), out_shape=(jax.S...  92.8 us
    pallas_call x1, Pallas kernels, local(): pl.pallas_call(functools.partial(gather_kernel, n, bits), out_shape=(jax....  39.7 us
    pallas_call x1, Pallas kernels, local(): pl.pallas_call(block_kernel, out_shape=(jax.ShapeDtypeStruct((REACH, poin...  13.2 us
    convert_element_type x1, other arithmetic, local(): posterior = (masked - noise_var[None, None, :] * precision).astype(BF16)  3.18 us

profile of v3, /device:TPU:0, one launch (start us, length us, event | category | flops | bytes accessed | tf_op | source)
XLA Modules:
  0.0 152.5 jit_solution(3742750869950556628)
XLA Ops:
  0.6 0.0 copy-start.4
  0.6 39.7 %shard_map.103 = (bf16[15,256,512]{2,1,0:T(8,128)(2,1)}, f32[6,256,512]{2,1,0:T(8,128)}) custom-call(s32[6]{0:T(128)} %counts.3, bf16[6,256,512]{2,1,0:T(8,128)(2,1)} %obs.1, bf16[6,256,2048]{2,1,0:T(8,128)(2,1)} %load.1, bf16[128,512]{1,0:T(8,128)(2,1)} %values.1), custom_call_target="tpu_custom_call" | custom-call | tf_op jit(solution)/shard_map/pallas_call | solution.py:435
  40.4 0.0 copy-done.4
  40.4 0.7 copy.11.near
  41.1 13.2 %shard_map.104 = (bf16[9,256,512]{2,1,0:T(8,128)(2,1)}, bf16[6,256,512]{2,1,0:T(8,128)(2,1)}, f32[6,256,512]{2,1,0:T(8,128)}, f32[8,512]{1,0:T(8,128)}) custom-call(s32[6,4]{1,0:T(8,128)} %copy.11.near, s32[6]{0:T(128)} %counts.3, bf16[15,256,512]{2,1,0:T(8,128)(2,1)} %get-tuple-element.12.window, f32[6,256,512]{2,1,0:T(8,128)} %get-tuple-element.13.base, ...), custom_call_target="tpu_custom_call" | custom-call | tf_op jit(solution)/shard_map/pallas_call | solution.py:463
  54.3 0.0 copy-start.2
  54.3 0.0 copy-start
  54.3 0.0 copy-start.3
  54.3 92.8 %shard_map.105 = (f32[6,256,512]{2,1,0:T(8,128)}, f32[8,512]{1,0:T(8,128)}, f32[128,512]{1,0:T(8,128)}) custom-call(f32[8,512]{1,0:T(8,128)} %get-tuple-element.14.stats, bf16[1536,512]{1,0:T(8,128)(2,1)} %bitcast.4, bf16[9,256,512]{2,1,0:T(8,128)(2,1)} %get-tuple-element.16.returned, f32[6,256,512]{2,1,0:T(8,128)} %get-tuple-element.17.rest, ...), custom_call_target="tpu_custom_call" | custom-call | tf_op jit(solution)/shard_map/pallas_call | solution.py:496
  147.1 0.0 copy-done.2
  147.1 0.1 iota_compare_fusion
  147.1 0.0 copy-done
  147.1 0.0 copy-done.3
  147.2 0.0 copy-start.1
  147.2 3.2 %subtract_convert_fusion = bf16[6,256,512]{2,1,0:T(8,128)(2,1)} fusion(f32[6,256,512]{2,1,0:T(8,128)} %get-tuple-element.18, bf16[6,256,512]{2,1,0:T(8,128)(2,1)S(1)} %copy-done, f32[512]{0:T(512)S(1)} %copy-done.3, pred[6,256]{1,0:T(8,128)(4,1)S(1)} %iota_compare_fusion), kind=kLoop, calls=%fused_computation | loop fusion | flops 4718592 | bytes 6295040 | tf_op jit(solution)/shard_map/convert_element_type | solution.py:529
  150.3 1.4 slice_divide_fusion
  151.8 0.0 copy-done.1
  151.8 0.7 copy.13
Async XLA Ops:
  0.6 39.7 %copy-start.4 = (s32[6,4]{0,1:T(4,128)S(1)}, s32[6,4]{0,1:T(4,128)}, u32[]{:S(2)}) copy-start(s32[6,4]{0,1:T(4,128)} %param.10) | copy-start | bytes 292
  54.3 92.8 %copy-start.2 = (s32[6]{0:T(128)S(1)}, s32[6]{0:T(128)}, u32[]{:S(2)}) copy-start(s32[6]{0:T(128)} %counts.3) | copy-start | bytes 76
  54.3 92.9 %copy-start = (bf16[6,256,512]{2,1,0:T(8,128)(2,1)S(1)}, bf16[6,256,512]{2,1,0:T(8,128)(2,1)}, u32[]{:S(2)}) copy-start(bf16[6,256,512]{2,1,0:T(8,128)(2,1)} %obs.1) | copy-start | bytes 4718596
  54.3 92.9 %copy-start.3 = (f32[512]{0:T(512)S(1)}, f32[512]{0:T(512)}, u32[]{:S(2)}) copy-start(f32[512]{0:T(512)} %param.15) | copy-start | bytes 6148
  147.2 4.6 %copy-start.1 = (f32[128,512]{1,0:T(8,128)S(1)}, f32[128,512]{1,0:T(8,128)}, u32[]{:S(2)}) copy-start(f32[128,512]{1,0:T(8,128)} %get-tuple-element.26) | copy-start | bytes 786436

commit v4 on v3

--- a/solution.py
+++ b/solution.py
@@ -324,11 +324,38 @@
     def start_of(t):
         return n - (n >> t)
 
-    def part_copy(t, j, m):
-        at = start_of(t) + m
+    mine = [lax.rem(i // (1 << b), 2) for b in range(bits)]
+    cut = fields - max(fields // 4, 128)
+    columns = [pl.ds(0, cut), pl.ds(cut, fields - cut)]
+    orders = [list(range(bits)), [0] + list(range(2, bits)) + [1]]
+    halves = range(len(orders))
+
+    def number(values, places):
+        total = 0
+        for k, b in enumerate(places):
+            total = total + values[b] * (1 << k)
+        return total
+
+    def place(h, t, values):
+        return start_of(t) + number(values, sorted(orders[h][t + 1 :]))
+
+    def part_copy(h, t, j, at):
         return remote(
-            partial.at[piece(j)], landed.at[at], part_send.at[at], part_recv.at[at], flip(i, t)
-        )
+            partial.at[piece(j), columns[h]],
+            landed.at[at, :, columns[h]],
+            part_send.at[h, at],
+            part_recv.at[h, at],
+            flip(i, orders[h][t]),
+        )
+
+    def sent(h, t):
+        free = sorted(orders[h][t + 1 :])
+        for m in range(1 << len(free)):
+            values = list(mine)
+            values[orders[h][t]] = 1 - mine[orders[h][t]]
+            for k, b in enumerate(free):
+                values[b] = (m >> k) % 2
+            yield values
 
     stat_copy(0).start()
     load_copy.wait()
@@ -345,36 +372,45 @@
         )
         for q in range(pairs):
             m = u * pairs + q
-            part_copy(0, 2 * m + other, m).start()
+            for h in halves:
+                part_copy(h, 0, 2 * m + other, m).start()
         return carry
 
     lax.fori_loop(0, knot_count // tile, tile_step, 0)
 
-    def settle(j, steps):
+    def settle(h, values, steps):
+        j = number(values, range(bits))
         for t in range(steps):
-            m = j // (2 << t)
-            at = start_of(t) + m
-            part_copy(t, j, m).wait_recv()
-            partial[piece(j), :] += landed[at]
+            at = place(h, t, values)
+            part_copy(h, t, j, at).wait_recv()
+            partial[piece(j), columns[h]] += landed[at, :, columns[h]]
+        return j
 
     for t in range(1, bits + 1):
         stat_copy(t - 1).wait_recv()
         stat_v[t] = stat_v[t - 1] + stat_in[t - 1]
         if t < bits:
             stat_copy(t).start()
-            low = lax.rem(flip(i, t), 2 << t)
-            for m in range(n >> (t + 1)):
-                j = low + m * (2 << t)
-                settle(j, t)
-                part_copy(t, j, m).start()
-        if t == 2:
-
-            @pl.when(i > 0)
+            for h in halves:
+                for values in sent(h, t):
+                    j = settle(h, values, t)
+                    part_copy(h, t, j, place(h, t, values)).start()
+        if t == 1:
+
+            @pl.when(lax.rem(i, 2) == 1)
             def _():
                 for s in reversed(range(slots)):
                     near_copy(s).start()
 
-    settle(i, bits)
+        if t == 2:
+
+            @pl.when(jnp.logical_and(i > 0, lax.rem(i, 2) == 0))
+            def _():
+                for s in reversed(range(slots)):
+                    near_copy(s).start()
+
+    for h in halves:
+        settle(h, mine, bits)
     score[...] = partial[piece(i), :]
     totals[...] = stat_v[bits]
 
@@ -405,9 +441,9 @@
 
     for t in range(bits):
         stat_copy(t).wait_send()
-        low = lax.rem(flip(i, t), 2 << t)
-        for m in range(n >> (t + 1)):
-            part_copy(t, low + m * (2 << t), m).wait_send()
+        for h in halves:
+            for values in sent(h, t):
+                part_copy(h, t, number(values, range(bits)), place(h, t, values)).wait_send()
 
 
 def vmem():
@@ -511,7 +547,7 @@
             pltpu.VMEM((bits + 1, 8, fields), F32),
             pltpu.VMEM((bits, 8, fields), F32),
             dma((2,)), dma((slots,)), dma((slots,)), dma((far,)), dma((far,)),
-            dma((n - 1,)), dma((n - 1,)), dma((bits,)), dma((bits,)),
+            dma((2, n - 1)), dma((2, n - 1)), dma((bits,)), dma((bits,)),
         ],
         compiler_params=pltpu.CompilerParams(
             collective_id=1, has_side_effects=True, vmem_limit_bytes=VMEM_LIMIT

time: 153 us -> 150 us (0.980)
  Pallas kernels: 146 us -> 143 us
    pallas_call x1, Pallas kernels: 92.8 us -> 89.9 us  [local(): pl.pallas_call(functools.partial(score_kernel, n, bits), out_shape=(jax.S...]
where the time goes in v4:
time: 150 us
  Pallas kernels  143 us (95%)
  other arithmetic  4.67 us (3%)
    pallas_call x1, Pallas kernels, local(): pl.pallas_call(functools.partial(score_kernel, n, bits), out_shape=(jax.S...  89.9 us
    pallas_call x1, Pallas kernels, local(): pl.pallas_call(functools.partial(gather_kernel, n, bits), out_shape=(jax....  39.7 us
    pallas_call x1, Pallas kernels, local(): pl.pallas_call(block_kernel, out_shape=(jax.ShapeDtypeStruct((REACH, poin...  13.2 us
    convert_element_type x1, other arithmetic, local(): posterior = (masked - noise_var[None, None, :] * precision).astype(BF16)  3.18 us

profile of v4, /device:TPU:0, one launch (start us, length us, event | category | flops | bytes accessed | tf_op | source)
XLA Modules:
  0.0 149.6 jit_solution(11265364459180457287)
XLA Ops:
  0.6 0.0 copy-start.4
  0.6 39.7 %shard_map.103 = (bf16[15,256,512]{2,1,0:T(8,128)(2,1)}, f32[6,256,512]{2,1,0:T(8,128)}) custom-call(s32[6]{0:T(128)} %counts.3, bf16[6,256,512]{2,1,0:T(8,128)(2,1)} %obs.1, bf16[6,256,2048]{2,1,0:T(8,128)(2,1)} %load.1, bf16[128,512]{1,0:T(8,128)(2,1)} %values.1), custom_call_target="tpu_custom_call" | custom-call | tf_op jit(solution)/shard_map/pallas_call | solution.py:471
  40.4 0.0 copy-done.4
  40.4 0.7 copy.11.near
  41.1 13.2 %shard_map.104 = (bf16[9,256,512]{2,1,0:T(8,128)(2,1)}, bf16[6,256,512]{2,1,0:T(8,128)(2,1)}, f32[6,256,512]{2,1,0:T(8,128)}, f32[8,512]{1,0:T(8,128)}) custom-call(s32[6,4]{1,0:T(8,128)} %copy.11.near, s32[6]{0:T(128)} %counts.3, bf16[15,256,512]{2,1,0:T(8,128)(2,1)} %get-tuple-element.12.window, f32[6,256,512]{2,1,0:T(8,128)} %get-tuple-element.13.base, ...), custom_call_target="tpu_custom_call" | custom-call | tf_op jit(solution)/shard_map/pallas_call | solution.py:499
  54.3 0.0 copy-start.2
  54.3 0.0 copy-start
  54.3 0.0 copy-start.3
  54.3 89.9 %shard_map.105 = (f32[6,256,512]{2,1,0:T(8,128)}, f32[8,512]{1,0:T(8,128)}, f32[128,512]{1,0:T(8,128)}) custom-call(f32[8,512]{1,0:T(8,128)} %get-tuple-element.14.stats, bf16[1536,512]{1,0:T(8,128)(2,1)} %bitcast.4, bf16[9,256,512]{2,1,0:T(8,128)(2,1)} %get-tuple-element.16.returned, f32[6,256,512]{2,1,0:T(8,128)} %get-tuple-element.17.rest, ...), custom_call_target="tpu_custom_call" | custom-call | tf_op jit(solution)/shard_map/pallas_call | solution.py:532
  144.2 0.0 copy-done.2
  144.2 0.1 iota_compare_fusion
  144.2 0.0 copy-done
  144.3 0.0 copy-done.3
  144.3 0.0 copy-start.1
  144.3 3.2 %subtract_convert_fusion = bf16[6,256,512]{2,1,0:T(8,128)(2,1)} fusion(f32[6,256,512]{2,1,0:T(8,128)} %get-tuple-element.18, bf16[6,256,512]{2,1,0:T(8,128)(2,1)S(1)} %copy-done, f32[512]{0:T(512)S(1)} %copy-done.3, pred[6,256]{1,0:T(8,128)(4,1)S(1)} %iota_compare_fusion), kind=kLoop, calls=%fused_computation | loop fusion | flops 4718592 | bytes 6295040 | tf_op jit(solution)/shard_map/convert_element_type | solution.py:565
  147.4 1.4 slice_divide_fusion
  148.9 0.0 copy-done.1
  148.9 0.7 copy.13
Async XLA Ops:
  0.6 39.7 %copy-start.4 = (s32[6,4]{0,1:T(4,128)S(1)}, s32[6,4]{0,1:T(4,128)}, u32[]{:S(2)}) copy-start(s32[6,4]{0,1:T(4,128)} %param.10) | copy-start | bytes 292
  54.3 89.9 %copy-start.2 = (s32[6]{0:T(128)S(1)}, s32[6]{0:T(128)}, u32[]{:S(2)}) copy-start(s32[6]{0:T(128)} %counts.3) | copy-start | bytes 76
  54.3 90.0 %copy-start = (bf16[6,256,512]{2,1,0:T(8,128)(2,1)S(1)}, bf16[6,256,512]{2,1,0:T(8,128)(2,1)}, u32[]{:S(2)}) copy-start(bf16[6,256,512]{2,1,0:T(8,128)(2,1)} %obs.1) | copy-start | bytes 4718596
  54.3 90.0 %copy-start.3 = (f32[512]{0:T(512)S(1)}, f32[512]{0:T(512)}, u32[]{:S(2)}) copy-start(f32[512]{0:T(512)} %param.15) | copy-start | bytes 6148
  144.3 4.6 %copy-start.1 = (f32[128,512]{1,0:T(8,128)S(1)}, f32[128,512]{1,0:T(8,128)}, u32[]{:S(2)}) copy-start(f32[128,512]{1,0:T(8,128)} %get-tuple-element.26) | copy-start | bytes 786436
